TPU v7x, 32 devices: a whole 2x2x4 slice. The times are simulated.
32 devices in a mesh: section: 4 (over x, core), expert: 8 (over z, y).
Axes of the slice: x: 2, y: 2, z: 4, core: 2. Of those that a mesh axis runs over, the one named last changes fastest.
Arguments:
- tokens: bfloat16 [8, 576, 2048], P(None, 'expert'), may hold values from -6 to 6
- w_in: bfloat16 [4, 2048, 2048], P('section', 'expert'), may hold values from -0.125 to 0.125
- w_out: bfloat16 [4, 2048, 2048], P('section', 'expert'), may hold values from -0.125 to 0.125
- router: bfloat16 [2048, 8], replicated, may hold values from -0.125 to 0.125
- exp_in: bfloat16 [8, 2048, 2048], P('expert', None, 'section'), may hold values from -0.125 to 0.125
- exp_out: bfloat16 [8, 2048, 2048], P('expert', 'section'), may hold values from -0.375 to 0.375
- active_rows: int32 [1152], P('expert'), may hold values from 0 to 575, as said below
- active_expert: int32 [1152, 1], P('expert'), may hold values from 0 to 7; in each aligned block of 144 rows (0 to 143, 144 to 287, ...) at most 54 rows name the same one
Outputs:
- updated: bfloat16 [8, 576, 2048], P(None, 'expert', 'section')
Inputs may be any that keep to these rules, and one draw needn't show every extreme that they name: `active_rows`: the 144 entries of one token block name distinct rows of its 576 rows. `active_expert`: among the 144 entries of one token block no expert is named more than 54 times.
All inputs are finite; a program needn't handle non-finite values.
Results may differ from a plain program's by a relative error of at most 0.024.
Values may be sent and summed in bfloat16 or wider, within the bound.
A program may use at most 64 MiB of HBM per device.

v0:
```python
import jax
import jax.numpy as jnp
from jax import lax
from jax.sharding import PartitionSpec as P


def from_behind(value, axis, steps):
    count = lax.axis_size(axis)
    initial, last = (max(0, -steps), min(count, count - steps))
    return lax.ppermute(value, axis, [(source, source + steps) for source in range(initial, last)])


def spread(shard, axis, root):
    mine = lax.axis_index(axis) == root
    return lax.psum(jnp.where(mine, shard, jnp.zeros_like(shard)), axis)


def normalize(rows):
    wide = rows.astype(jnp.float32)
    scale = lax.rsqrt(jnp.mean(wide * wide, axis=-1, keepdims=True) + 1e-05)
    return wide * scale


def processor(stream, w_first, w_second):
    normed = normalize(stream).astype(jnp.bfloat16)
    hidden = jax.nn.silu(jnp.dot(normed, w_first, preferred_element_type=jnp.float32)).astype(
        jnp.bfloat16
    )
    branch = jnp.dot(hidden, w_second, preferred_element_type=jnp.float32)
    return (stream.astype(jnp.float32) + branch).astype(jnp.bfloat16)


def local(tokens, w_in, w_out, router, exp_in, exp_out, active_rows, active_expert):
    n_section = lax.axis_size("section")
    section = lax.axis_index("section")
    micro, tok_dev, width = tokens.shape
    w_first, w_second = (
        lax.all_gather(w_in, "expert", axis=1, tiled=True),
        lax.all_gather(w_out, "expert", axis=1, tiled=True),
    )
    w_first = w_first[0]
    w_second = w_second[0]
    last = n_section - 1

    def run_layer(stream):
        return processor(stream, w_first, w_second)

    def skip_layer(stream):
        return jnp.zeros_like(stream)

    def tick(step, carry):
        incoming, collected = carry
        micro_index = step - section
        valid = (micro_index >= 0) & (micro_index < micro)
        clamped = jnp.clip(micro_index, 0, micro - 1)
        fresh = lax.dynamic_index_in_dim(tokens, clamped, 0, keepdims=False)
        stream = jnp.where(section == 0, fresh, incoming)
        result = lax.cond(valid, run_layer, skip_layer, stream)
        updated = lax.dynamic_update_index_in_dim(collected, result, clamped, 0)
        collected = jnp.where(valid & (section == last), updated, collected)
        passed = from_behind(result, "section", 1)
        return (passed, collected)

    start = (jnp.zeros((tok_dev, width), jnp.bfloat16), jnp.zeros_like(tokens))
    passed, collected = lax.fori_loop(0, micro + n_section - 1, tick, start)
    final = spread(collected, "section", last)
    rows_dev = micro * tok_dev
    flat = final.reshape(rows_dev, width)
    n_exp = router.shape[1]
    act_dev = active_rows.shape[0]
    capacity = 3 * act_dev // n_exp
    picked = jnp.take(flat, active_rows, axis=0)
    contact = normalize(picked).astype(jnp.bfloat16)
    chosen = active_expert[:, 0]
    onehot = chosen[:, None] == jnp.arange(n_exp, dtype=jnp.int32)[None, :]
    logits = jnp.dot(contact, router, preferred_element_type=jnp.float32)
    gate = jax.nn.sigmoid(jnp.sum(jnp.where(onehot, logits, 0.0), axis=1))
    counts = onehot.astype(jnp.int32)
    earlier = jnp.cumsum(counts, axis=0) - counts
    rank = jnp.sum(earlier * counts, axis=1)
    position = chosen * capacity + rank
    placing = (jnp.arange(n_exp * capacity, dtype=jnp.int32)[:, None] == position[None, :]).astype(
        jnp.bfloat16
    )
    outgoing = jnp.dot(placing, contact, preferred_element_type=jnp.float32).astype(jnp.bfloat16)
    outgoing = outgoing.reshape(n_exp, capacity, width)
    e_first = exp_in[0]
    e_second = exp_out[0]
    arrived = lax.all_to_all(outgoing, "expert", split_axis=0, concat_axis=0, tiled=True)
    sources, slots, _ = arrived.shape
    rows = arrived.reshape(sources * slots, width)
    hidden = jax.nn.silu(jnp.dot(rows, e_first, preferred_element_type=jnp.float32)).astype(
        jnp.bfloat16
    )
    partial_value = jnp.dot(hidden, e_second, preferred_element_type=jnp.float32).reshape(
        sources, slots, width
    )
    part_width = width // n_section
    returned = lax.all_to_all(
        partial_value.astype(jnp.bfloat16), "expert", split_axis=0, concat_axis=0, tiled=True
    ).astype(partial_value.dtype)
    mine = jnp.take(returned.reshape(n_exp * capacity, width), position, axis=0)
    added = lax.psum_scatter(
        (gate[:, None] * mine).astype(jnp.bfloat16), "section", scatter_dimension=1, tiled=True
    ).astype(jnp.float32)
    base = lax.dynamic_slice_in_dim(flat, section * part_width, part_width, 1).astype(jnp.float32)
    mixed = base.at[active_rows].add(added)
    return mixed.astype(jnp.bfloat16).reshape(micro, tok_dev, part_width)


def solution(mesh):
    return jax.shard_map(
        local,
        mesh=mesh,
        in_specs=(
            P(None, "expert", None),
            P("section", "expert", None),
            P("section", "expert", None),
            P(),
            P("expert", None, "section"),
            P("expert", "section", None),
            P("expert"),
            P("expert", None),
        ),
        out_specs=P(None, "expert", "section"),
        check_vma=False,
    )
```

profile of v0, /device:TPU:0, one launch (start us, length us, event | category | flops | bytes accessed | tf_op | source)
XLA Modules:
  0.0 682.6 jit_solution(6736409796696927758)
XLA Ops:
  8.7 128.5 %all-gather.3.cloned.1.call-done = bf16[1,2048,2048]{2,1,0:T(8,128)(2,1)} async-done(((bf16[1,256,2048]{2,1,0:T(8,128)(2,1)}), bf16[1,2048,2048]{2,1,0:T(8,128)(2,1)}) %all-gather.3.cloned.1.call-update) | async-done | bytes 8388624 | tf_op jit(solution)/shard_map/all_gather | solution.py:38
  137.2 125.3 %all-gather.5.cloned.1.call-done = bf16[1,2048,2048]{2,1,0:T(8,128)(2,1)} async-done(((bf16[1,256,2048]{2,1,0:T(8,128)(2,1)}), bf16[1,2048,2048]{2,1,0:T(8,128)(2,1)}) %all-gather.5.cloned.1.call-update) | async-done | bytes 8388624 | tf_op jit(solution)/shard_map/all_gather | solution.py:39
  264.2 197.9 %while.16 = (s32[]{:T(128)}, bf16[72,2048]{1,0:T(8,128)(2,1)S(1)}, bf16[8,72,2048]{2,1,0:T(8,128)(2,1)}, s32[]{:T(128)}, pred[]{:T(512)}, /*index=5*/bf16[8,72,2...) while((s32[]{:T(128)}, bf16[72,2048]{1,0:T(8,128)(2,1)S(1)}, ...), condition=%wide.region_4.5_spmd, body=%wide.region_0.4_spmd.sunk | while | flops 1210613888 | bytes 21500040 | solution.py:65
  264.2 11.9 %conditional.2 = (bf16[72,2048]{1,0:T(8,128)(2,1)}, bf16[1,72,2048]{2,1,0:T(8,128)(2,1)S(1)}) conditional(s32[]{:T(128)} %convert_element_type.109, () %tuple.47, (pred[]{:T(512)}, bf16[8,72,2048]{2,1,0:T(8,128)(2,1)}, s32[]{:T(128)}, bf16[72,2048]{1,0:T(8,128)(2,1)S(1)}, bf16[2048,2048]{1,0:T(8,128)(2,1)}, ...), branch_computations={%region_1.1_spmd, %region_2.3_spmd} | conditional | flops 1210466432 | bytes 19434868 | solution.py:58
  265.4 9.7 %fusion = bf16[72,2048]{1,0:T(8,128)(2,1)} fusion(bf16[2048,2048]{1,0:T(8,128)(2,1)} %get-tuple-element.195, bf16[2048,2048]{1,0:T(8,128)(2,1)} %get-tuple-element.194, f32[72]{0:T(128)S(1)} %add_rsqrt_fusion, bf16[72,2048]{1,0:T(8,128)(2,1)S(1)} %get-tuple-element.193, bf16[8,72,2048]{2,1,0:T(8,128)(2,1)} %get-tuple-element.191, s32[]{:T(128)} %get-tuple-element.192, ...), kind=kOutput, calls=%fused_computation.4 | convolution fusion | flops 1209876480 | bytes 18254336 | tf_op jit(solution)/shard_map/while/body/eval_jaxpr/cond/branch_1_fun/dot_general | solution.py:29
  279.1 11.8 %conditional.2 = (bf16[72,2048]{1,0:T(8,128)(2,1)}, bf16[1,72,2048]{2,1,0:T(8,128)(2,1)S(1)}) conditional(s32[]{:T(128)} %convert_element_type.109, () %tuple.47, (pred[]{:T(512)}, bf16[8,72,2048]{2,1,0:T(8,128)(2,1)}, s32[]{:T(128)}, bf16[72,2048]{1,0:T(8,128)(2,1)S(1)}, bf16[2048,2048]{1,0:T(8,128)(2,1)}, ...), branch_computations={%region_1.1_spmd, %region_2.3_spmd} | conditional | flops 1210466432 | bytes 19434868 | solution.py:58
  280.3 9.7 %fusion = bf16[72,2048]{1,0:T(8,128)(2,1)} fusion(bf16[2048,2048]{1,0:T(8,128)(2,1)} %get-tuple-element.195, bf16[2048,2048]{1,0:T(8,128)(2,1)} %get-tuple-element.194, f32[72]{0:T(128)S(1)} %add_rsqrt_fusion, bf16[72,2048]{1,0:T(8,128)(2,1)S(1)} %get-tuple-element.193, bf16[8,72,2048]{2,1,0:T(8,128)(2,1)} %get-tuple-element.191, s32[]{:T(128)} %get-tuple-element.192, ...), kind=kOutput, calls=%fused_computation.4 | convolution fusion | flops 1209876480 | bytes 18254336 | tf_op jit(solution)/shard_map/while/body/eval_jaxpr/cond/branch_1_fun/dot_general | solution.py:29
  294.6 11.8 %conditional.2 = (bf16[72,2048]{1,0:T(8,128)(2,1)}, bf16[1,72,2048]{2,1,0:T(8,128)(2,1)S(1)}) conditional(s32[]{:T(128)} %convert_element_type.109, () %tuple.47, (pred[]{:T(512)}, bf16[8,72,2048]{2,1,0:T(8,128)(2,1)}, s32[]{:T(128)}, bf16[72,2048]{1,0:T(8,128)(2,1)S(1)}, bf16[2048,2048]{1,0:T(8,128)(2,1)}, ...), branch_computations={%region_1.1_spmd, %region_2.3_spmd} | conditional | flops 1210466432 | bytes 19434868 | solution.py:58
  295.8 9.7 %fusion = bf16[72,2048]{1,0:T(8,128)(2,1)} fusion(bf16[2048,2048]{1,0:T(8,128)(2,1)} %get-tuple-element.195, bf16[2048,2048]{1,0:T(8,128)(2,1)} %get-tuple-element.194, f32[72]{0:T(128)S(1)} %add_rsqrt_fusion, bf16[72,2048]{1,0:T(8,128)(2,1)S(1)} %get-tuple-element.193, bf16[8,72,2048]{2,1,0:T(8,128)(2,1)} %get-tuple-element.191, s32[]{:T(128)} %get-tuple-element.192, ...), kind=kOutput, calls=%fused_computation.4 | convolution fusion | flops 1209876480 | bytes 18254336 | tf_op jit(solution)/shard_map/while/body/eval_jaxpr/cond/branch_1_fun/dot_general | solution.py:29
  312.4 11.8 %conditional.2 = (bf16[72,2048]{1,0:T(8,128)(2,1)}, bf16[1,72,2048]{2,1,0:T(8,128)(2,1)S(1)}) conditional(s32[]{:T(128)} %convert_element_type.109, () %tuple.47, (pred[]{:T(512)}, bf16[8,72,2048]{2,1,0:T(8,128)(2,1)}, s32[]{:T(128)}, bf16[72,2048]{1,0:T(8,128)(2,1)S(1)}, bf16[2048,2048]{1,0:T(8,128)(2,1)}, ...), branch_computations={%region_1.1_spmd, %region_2.3_spmd} | conditional | flops 1210466432 | bytes 19434868 | solution.py:58
  313.5 9.7 %fusion = bf16[72,2048]{1,0:T(8,128)(2,1)} fusion(bf16[2048,2048]{1,0:T(8,128)(2,1)} %get-tuple-element.195, bf16[2048,2048]{1,0:T(8,128)(2,1)} %get-tuple-element.194, f32[72]{0:T(128)S(1)} %add_rsqrt_fusion, bf16[72,2048]{1,0:T(8,128)(2,1)S(1)} %get-tuple-element.193, bf16[8,72,2048]{2,1,0:T(8,128)(2,1)} %get-tuple-element.191, s32[]{:T(128)} %get-tuple-element.192, ...), kind=kOutput, calls=%fused_computation.4 | convolution fusion | flops 1209876480 | bytes 18254336 | tf_op jit(solution)/shard_map/while/body/eval_jaxpr/cond/branch_1_fun/dot_general | solution.py:29
  324.2 6.5 collective-permute-start
  332.5 11.8 %conditional.2 = (bf16[72,2048]{1,0:T(8,128)(2,1)}, bf16[1,72,2048]{2,1,0:T(8,128)(2,1)S(1)}) conditional(s32[]{:T(128)} %convert_element_type.109, () %tuple.47, (pred[]{:T(512)}, bf16[8,72,2048]{2,1,0:T(8,128)(2,1)}, s32[]{:T(128)}, bf16[72,2048]{1,0:T(8,128)(2,1)S(1)}, bf16[2048,2048]{1,0:T(8,128)(2,1)}, ...), branch_computations={%region_1.1_spmd, %region_2.3_spmd} | conditional | flops 1210466432 | bytes 19434868 | solution.py:58
  333.6 9.7 %fusion = bf16[72,2048]{1,0:T(8,128)(2,1)} fusion(bf16[2048,2048]{1,0:T(8,128)(2,1)} %get-tuple-element.195, bf16[2048,2048]{1,0:T(8,128)(2,1)} %get-tuple-element.194, f32[72]{0:T(128)S(1)} %add_rsqrt_fusion, bf16[72,2048]{1,0:T(8,128)(2,1)S(1)} %get-tuple-element.193, bf16[8,72,2048]{2,1,0:T(8,128)(2,1)} %get-tuple-element.191, s32[]{:T(128)} %get-tuple-element.192, ...), kind=kOutput, calls=%fused_computation.4 | convolution fusion | flops 1209876480 | bytes 18254336 | tf_op jit(solution)/shard_map/while/body/eval_jaxpr/cond/branch_1_fun/dot_general | solution.py:29
  344.3 6.5 collective-permute-start
  352.6 11.8 %conditional.2 = (bf16[72,2048]{1,0:T(8,128)(2,1)}, bf16[1,72,2048]{2,1,0:T(8,128)(2,1)S(1)}) conditional(s32[]{:T(128)} %convert_element_type.109, () %tuple.47, (pred[]{:T(512)}, bf16[8,72,2048]{2,1,0:T(8,128)(2,1)}, s32[]{:T(128)}, bf16[72,2048]{1,0:T(8,128)(2,1)S(1)}, bf16[2048,2048]{1,0:T(8,128)(2,1)}, ...), branch_computations={%region_1.1_spmd, %region_2.3_spmd} | conditional | flops 1210466432 | bytes 19434868 | solution.py:58
  353.7 9.7 %fusion = bf16[72,2048]{1,0:T(8,128)(2,1)} fusion(bf16[2048,2048]{1,0:T(8,128)(2,1)} %get-tuple-element.195, bf16[2048,2048]{1,0:T(8,128)(2,1)} %get-tuple-element.194, f32[72]{0:T(128)S(1)} %add_rsqrt_fusion, bf16[72,2048]{1,0:T(8,128)(2,1)S(1)} %get-tuple-element.193, bf16[8,72,2048]{2,1,0:T(8,128)(2,1)} %get-tuple-element.191, s32[]{:T(128)} %get-tuple-element.192, ...), kind=kOutput, calls=%fused_computation.4 | convolution fusion | flops 1209876480 | bytes 18254336 | tf_op jit(solution)/shard_map/while/body/eval_jaxpr/cond/branch_1_fun/dot_general | solution.py:29
  364.4 6.5 collective-permute-start
  372.7 11.8 %conditional.2 = (bf16[72,2048]{1,0:T(8,128)(2,1)}, bf16[1,72,2048]{2,1,0:T(8,128)(2,1)S(1)}) conditional(s32[]{:T(128)} %convert_element_type.109, () %tuple.47, (pred[]{:T(512)}, bf16[8,72,2048]{2,1,0:T(8,128)(2,1)}, s32[]{:T(128)}, bf16[72,2048]{1,0:T(8,128)(2,1)S(1)}, bf16[2048,2048]{1,0:T(8,128)(2,1)}, ...), branch_computations={%region_1.1_spmd, %region_2.3_spmd} | conditional | flops 1210466432 | bytes 19434868 | solution.py:58
  373.8 9.7 %fusion = bf16[72,2048]{1,0:T(8,128)(2,1)} fusion(bf16[2048,2048]{1,0:T(8,128)(2,1)} %get-tuple-element.195, bf16[2048,2048]{1,0:T(8,128)(2,1)} %get-tuple-element.194, f32[72]{0:T(128)S(1)} %add_rsqrt_fusion, bf16[72,2048]{1,0:T(8,128)(2,1)S(1)} %get-tuple-element.193, bf16[8,72,2048]{2,1,0:T(8,128)(2,1)} %get-tuple-element.191, s32[]{:T(128)} %get-tuple-element.192, ...), kind=kOutput, calls=%fused_computation.4 | convolution fusion | flops 1209876480 | bytes 18254336 | tf_op jit(solution)/shard_map/while/body/eval_jaxpr/cond/branch_1_fun/dot_general | solution.py:29
  384.5 6.5 collective-permute-start
  392.7 11.8 %conditional.2 = (bf16[72,2048]{1,0:T(8,128)(2,1)}, bf16[1,72,2048]{2,1,0:T(8,128)(2,1)S(1)}) conditional(s32[]{:T(128)} %convert_element_type.109, () %tuple.47, (pred[]{:T(512)}, bf16[8,72,2048]{2,1,0:T(8,128)(2,1)}, s32[]{:T(128)}, bf16[72,2048]{1,0:T(8,128)(2,1)S(1)}, bf16[2048,2048]{1,0:T(8,128)(2,1)}, ...), branch_computations={%region_1.1_spmd, %region_2.3_spmd} | conditional | flops 1210466432 | bytes 19434868 | solution.py:58
  393.9 9.7 %fusion = bf16[72,2048]{1,0:T(8,128)(2,1)} fusion(bf16[2048,2048]{1,0:T(8,128)(2,1)} %get-tuple-element.195, bf16[2048,2048]{1,0:T(8,128)(2,1)} %get-tuple-element.194, f32[72]{0:T(128)S(1)} %add_rsqrt_fusion, bf16[72,2048]{1,0:T(8,128)(2,1)S(1)} %get-tuple-element.193, bf16[8,72,2048]{2,1,0:T(8,128)(2,1)} %get-tuple-element.191, s32[]{:T(128)} %get-tuple-element.192, ...), kind=kOutput, calls=%fused_computation.4 | convolution fusion | flops 1209876480 | bytes 18254336 | tf_op jit(solution)/shard_map/while/body/eval_jaxpr/cond/branch_1_fun/dot_general | solution.py:29
  404.6 6.5 collective-permute-start
  413.6 17.5 %collective-permute-start = (bf16[72,2048]{1,0:T(8,128)(2,1)}, bf16[72,2048]{1,0:T(8,128)(2,1)S(1)}, u32[]{:S(2)}, u32[]{:S(2)}) collective-permute-start(bf16[72,2048]{1,0:T(8,128)(2,1)} %get-tuple-element.287), channel_id=1, source_target_pairs={{0,8},{8,16},{16,24},{1,9},{9,17},{17,25},{2,10},{10,18},{18,26},{... | collective-permute-start | bytes 884744 | tf_op jit(solution)/shard_map/while/body/eval_jaxpr/ppermute | solution.py:10
  433.7 6.5 collective-permute-start
  442.7 17.5 %collective-permute-start = (bf16[72,2048]{1,0:T(8,128)(2,1)}, bf16[72,2048]{1,0:T(8,128)(2,1)S(1)}, u32[]{:S(2)}, u32[]{:S(2)}) collective-permute-start(bf16[72,2048]{1,0:T(8,128)(2,1)} %get-tuple-element.287), channel_id=1, source_target_pairs={{0,8},{8,16},{16,24},{1,9},{9,17},{17,25},{2,10},{10,18},{18,26},{... | collective-permute-start | bytes 884744 | tf_op jit(solution)/shard_map/while/body/eval_jaxpr/ppermute | solution.py:10
  464.4 61.8 %all-reduce.3.cloned.1.call-done = bf16[576,2048]{1,0:T(8,128)(2,1)} async-done(((bf16[576,2048]{1,0:T(8,128)(2,1)}), bf16[576,2048]{1,0:T(8,128)(2,1)}) %all-reduce.3.cloned.1.call-update) | async-done | bytes 2359312 | tf_op jit(solution)/shard_map/psum | solution.py:15
  534.7 48.2 %all_to_all.10 = bf16[8,54,2048]{2,1,0:T(8,128)(2,1)} all-to-all(bf16[8,54,2048]{2,1,0:T(8,128)(2,1)} %reshape.75), channel_id=1, replica_groups=mesh['section'=4,'expert'=8] {'expert'}, dimensions={0} | all-to-all | bytes 3538944 | tf_op jit(solution)/shard_map/all_to_all | solution.py:89
  598.1 41.3 %all-to-all-done.1 = bf16[8,54,2048]{2,1,0:T(8,128)(2,1)} async-done(((bf16[8,54,2048]{2,1,0:T(8,128)(2,1)}), bf16[8,54,2048]{2,1,0:T(8,128)(2,1)}, u32[]{:S(2)}, u32[]{:S(2)}) %all-to-all-start.1) | async-done | bytes 1769504 | tf_op jit(solution)/shard_map/all_to_all | solution.py:99
  642.5 4.5 gather_fusion.1
  651.6 18.3 %reduce-scatter.2.cloned.1.call-done = bf16[144,512]{1,0:T(8,128)(2,1)} async-done(((bf16[144,2048]{1,0:T(8,128)(2,1)}), bf16[144,512]{1,0:T(8,128)(2,1)}) %reduce-scatter.2.cloned.1.call-update) | async-done | bytes 147472 | tf_op jit(solution)/shard_map/reduce_scatter | solution.py:103
  (108 shorter events, 92.0 us)
Async XLA Ops:
  6.5 584.2 %copy-start = (bf16[1,512,2048]{2,1,0:T(8,128)(2,1)S(1)}, bf16[1,512,2048]{2,1,0:T(8,128)(2,1)}, u32[]{:S(2)}) copy-start(bf16[1,512,2048]{2,1,0:T(8,128)(2,1)} %param.17) | copy-start | bytes 6291460
  6.5 1.5 copy-start.1
  6.5 130.6 %all-gather.3.cloned.1.call-start = ((), (), s32[]{:S(2)}) async-start(), calls=%async_computation.3 | async-start | bytes 9437184 | tf_op jit(solution)/shard_map/all_gather | solution.py:38
  7.3 255.2 %all-gather.5.cloned.1.call-start = ((), (), s32[]{:S(2)}) async-start(), calls=%async_computation.4 | async-start | bytes 9437184 | tf_op jit(solution)/shard_map/all_gather | solution.py:39
  8.0 518.2 %all-reduce.3.cloned.1.call-start = ((), (), s32[]{:S(2)}) async-start(), calls=%async_computation.5 | async-start | bytes 4718592 | tf_op jit(solution)/shard_map/psum | solution.py:15
  276.1 3.1 collective-permute-start
  291.0 3.7 collective-permute-start
  306.5 5.9 collective-permute-start
  324.2 8.2 %collective-permute-start = (bf16[72,2048]{1,0:T(8,128)(2,1)}, bf16[72,2048]{1,0:T(8,128)(2,1)S(1)}, u32[]{:S(2)}, u32[]{:S(2)}) collective-permute-start(bf16[72,2048]{1,0:T(8,128)(2,1)} %get-tuple-element.287), channel_id=1, source_target_pairs={{0,8},{8,16},{16,24},{1,9},{9,17},{17,25},{2,10},{10,18},{18,26},{... | collective-permute-start | bytes 884744 | tf_op jit(solution)/shard_map/while/body/eval_jaxpr/ppermute | solution.py:10
  344.3 8.3 %collective-permute-start = (bf16[72,2048]{1,0:T(8,128)(2,1)}, bf16[72,2048]{1,0:T(8,128)(2,1)S(1)}, u32[]{:S(2)}, u32[]{:S(2)}) collective-permute-start(bf16[72,2048]{1,0:T(8,128)(2,1)} %get-tuple-element.287), channel_id=1, source_target_pairs={{0,8},{8,16},{16,24},{1,9},{9,17},{17,25},{2,10},{10,18},{18,26},{... | collective-permute-start | bytes 884744 | tf_op jit(solution)/shard_map/while/body/eval_jaxpr/ppermute | solution.py:10
  364.4 8.2 %collective-permute-start = (bf16[72,2048]{1,0:T(8,128)(2,1)}, bf16[72,2048]{1,0:T(8,128)(2,1)S(1)}, u32[]{:S(2)}, u32[]{:S(2)}) collective-permute-start(bf16[72,2048]{1,0:T(8,128)(2,1)} %get-tuple-element.287), channel_id=1, source_target_pairs={{0,8},{8,16},{16,24},{1,9},{9,17},{17,25},{2,10},{10,18},{18,26},{... | collective-permute-start | bytes 884744 | tf_op jit(solution)/shard_map/while/body/eval_jaxpr/ppermute | solution.py:10
  384.5 8.2 %collective-permute-start = (bf16[72,2048]{1,0:T(8,128)(2,1)}, bf16[72,2048]{1,0:T(8,128)(2,1)S(1)}, u32[]{:S(2)}, u32[]{:S(2)}) collective-permute-start(bf16[72,2048]{1,0:T(8,128)(2,1)} %get-tuple-element.287), channel_id=1, source_target_pairs={{0,8},{8,16},{16,24},{1,9},{9,17},{17,25},{2,10},{10,18},{18,26},{... | collective-permute-start | bytes 884744 | tf_op jit(solution)/shard_map/while/body/eval_jaxpr/ppermute | solution.py:10
  404.6 8.2 %collective-permute-start = (bf16[72,2048]{1,0:T(8,128)(2,1)}, bf16[72,2048]{1,0:T(8,128)(2,1)S(1)}, u32[]{:S(2)}, u32[]{:S(2)}) collective-permute-start(bf16[72,2048]{1,0:T(8,128)(2,1)} %get-tuple-element.287), channel_id=1, source_target_pairs={{0,8},{8,16},{16,24},{1,9},{9,17},{17,25},{2,10},{10,18},{18,26},{... | collective-permute-start | bytes 884744 | tf_op jit(solution)/shard_map/while/body/eval_jaxpr/ppermute | solution.py:10
  413.6 19.3 %collective-permute-start = (bf16[72,2048]{1,0:T(8,128)(2,1)}, bf16[72,2048]{1,0:T(8,128)(2,1)S(1)}, u32[]{:S(2)}, u32[]{:S(2)}) collective-permute-start(bf16[72,2048]{1,0:T(8,128)(2,1)} %get-tuple-element.287), channel_id=1, source_target_pairs={{0,8},{8,16},{16,24},{1,9},{9,17},{17,25},{2,10},{10,18},{18,26},{... | collective-permute-start | bytes 884744 | tf_op jit(solution)/shard_map/while/body/eval_jaxpr/ppermute | solution.py:10
  433.7 8.3 %collective-permute-start = (bf16[72,2048]{1,0:T(8,128)(2,1)}, bf16[72,2048]{1,0:T(8,128)(2,1)S(1)}, u32[]{:S(2)}, u32[]{:S(2)}) collective-permute-start(bf16[72,2048]{1,0:T(8,128)(2,1)} %get-tuple-element.287), channel_id=1, source_target_pairs={{0,8},{8,16},{16,24},{1,9},{9,17},{17,25},{2,10},{10,18},{18,26},{... | collective-permute-start | bytes 884744 | tf_op jit(solution)/shard_map/while/body/eval_jaxpr/ppermute | solution.py:10
  442.7 19.3 %collective-permute-start = (bf16[72,2048]{1,0:T(8,128)(2,1)}, bf16[72,2048]{1,0:T(8,128)(2,1)S(1)}, u32[]{:S(2)}, u32[]{:S(2)}) collective-permute-start(bf16[72,2048]{1,0:T(8,128)(2,1)} %get-tuple-element.287), channel_id=1, source_target_pairs={{0,8},{8,16},{16,24},{1,9},{9,17},{17,25},{2,10},{10,18},{18,26},{... | collective-permute-start | bytes 884744 | tf_op jit(solution)/shard_map/while/body/eval_jaxpr/ppermute | solution.py:10
  463.6 0.7 copy-start.2
  593.1 4.6 copy-start.3
  593.1 46.2 %all-to-all-start.1 = ((bf16[8,54,2048]{2,1,0:T(8,128)(2,1)}), bf16[8,54,2048]{2,1,0:T(8,128)(2,1)}, u32[]{:S(2)}, u32[]{:S(2)}) async-start(bf16[8,54,2048]{2,1,0:T(8,128)(2,1)} %convolution_convert_fusion), calls=%async_computation.1 | async-start | bytes 3670016 | tf_op jit(solution)/shard_map/all_to_all | solution.py:99
  597.6 72.3 %reduce-scatter.2.cloned.1.call-start = ((), (), s32[]{:S(2)}) async-start(), calls=%async_computation.6 | async-start | bytes 737280 | tf_op jit(solution)/shard_map/reduce_scatter | solution.py:103
Sparse Core Ops, SparseCore 0:
  9.5 127.6 all-gather.2
  139.3 123.1 all-gather.4
  463.8 62.3 all-reduce.2
  649.5 20.3 reduce-scatter.1
where the time goes:
time: 684 us; the launch traced here: 683 us
  waiting for transfers between devices  377 us (55%)
  matrix products  86.5 us (13%)
  starting transfers between devices  85.8 us (13%)
  blocking collectives  48.2 us (7%)
  other arithmetic  42 us (6%)
  local copies, waits for them, and re-layouts  30 us (4%)
  between operations  13.2 us (2%)
    all_gather x1, waiting for transfers between devices, local(): lax.all_gather(w_in, 'expert', axis=1, tiled=True)  128 us
    all_gather x1, waiting for transfers between devices, local(): lax.all_gather(w_out, 'expert', axis=1, tiled=True)  125 us
    ppermute x11, starting transfers between devices, from_behind(): lax.ppermute(value, axis, [(source, source + steps) for source in range(i...  81.2 us
    dot_general x8, matrix products, processor(): branch = jnp.dot(hidden, w_second, preferred_element_type=jnp.float32)  77.7 us
    psum x1, waiting for transfers between devices, spread(): return lax.psum(jnp.where(mine, shard, jnp.zeros_like(shard)), axis)  61.8 us
    all_to_all x1, blocking collectives, local(): lax.all_to_all(outgoing, 'expert', split_axis=0, concat_axis=0, tiled=True)  48.2 us
    all_to_all x1, waiting for transfers between devices, local(): lax.all_to_all(partial_value.astype(jnp.bfloat16), 'expert', split_axis=0...  41.3 us
    select_n x11, other arithmetic, tick(): collected = jnp.where(valid & (section == last), updated, collected)  19.3 us
  transfers between devices with their start and end apart: 16, of which 5 were waited for; matrix products, arithmetic and copies ran while one was open for 3% of the time, Pallas kernels for 0%

commit v1 on v0

v1 whole, which is shorter than its diff:
```python
import functools

import jax
import jax.numpy as jnp
from jax import lax
from jax.experimental import pallas as pl
from jax.experimental.pallas import tpu as pltpu
from jax.sharding import PartitionSpec as P

MESH = pl.DeviceIdType.MESH


def gather_kernel(n_z, n_y, first_ref, second_ref, first_out, second_out, local_sem, send_sem, recv_sem):
    me = lax.axis_index("expert")
    z, y = lax.div(me, n_y), lax.rem(me, n_y)
    rows = first_ref.shape[0]
    outs = (first_out, second_out)
    up, down, right, left = range(4)
    steps = (n_y, -n_y, 1, -1)
    there = (z < n_z - 1, z > 0, y < n_y - 1, y > 0)

    barrier = pltpu.get_barrier_semaphore()
    for way in range(4):

        @pl.when(there[way])
        def _(way=way):
            pl.semaphore_signal(barrier, inc=1, device_id={"expert": me + steps[way]}, device_id_type=MESH)

    pl.semaphore_wait(barrier, sum(near.astype(jnp.int32) for near in there))

    def block(which, owner):
        return outs[which].at[pl.ds(pl.multiple_of(owner * rows, rows), rows)]

    def copy(which, owner, way):
        return pltpu.make_async_remote_copy(
            src_ref=block(which, owner),
            dst_ref=block(which, owner),
            send_sem=send_sem.at[way, which, owner],
            recv_sem=recv_sem.at[which, owner],
            device_id={"expert": me + steps[way]},
            device_id_type=MESH,
        )

    def send(which, owner, ways, finish):
        for way in ways:

            @pl.when(there[way])
            def _(way=way):
                sent = copy(which, owner, way)
                if finish:
                    sent.wait_send()
                else:
                    sent.start()

    def visit(finish):
        for far in range(n_z):
            for which in range(2):
                for sign in (-1, 1) if far else (0,):
                    row = z + sign * far

                    @pl.when((row >= 0) & (row < n_z))
                    def _(which=which, row=row, sign=sign):
                        owner = row * n_y + y
                        if sign and not finish:
                            copy(which, owner, down if sign < 0 else up).wait_recv()
                        onward = {0: (up, down), -1: (up,), 1: (down,)}[sign]
                        send(which, owner, onward + (right, left), finish)

        for far in range(1, n_y):
            for row in range(n_z):
                for which in range(2):
                    for sign in (-1, 1):
                        column = y + sign * far

                        @pl.when((column >= 0) & (column < n_y))
                        def _(which=which, row=row, column=column, sign=sign):
                            owner = row * n_y + column
                            if not finish:
                                copy(which, owner, left if sign < 0 else right).wait_recv()
                            if n_y > 2:
                                send(which, owner, (right,) if sign < 0 else (left,), finish)

    own = [
        pltpu.make_async_copy(ref, block(which, me), local_sem.at[which])
        for which, ref in enumerate((first_ref, second_ref))
    ]
    for each in own:
        each.start()
    for each in own:
        each.wait()
    visit(False)
    visit(True)


def gather_weights(w_first, w_second, n_z, n_y):
    rows, width = w_first.shape
    whole = jax.ShapeDtypeStruct((n_z * n_y * rows, width), w_first.dtype)
    return pl.pallas_call(
        functools.partial(gather_kernel, n_z, n_y),
        out_shape=(whole, whole),
        in_specs=[pl.BlockSpec(memory_space=pl.ANY)] * 2,
        out_specs=(pl.BlockSpec(memory_space=pl.ANY), pl.BlockSpec(memory_space=pl.ANY)),
        scratch_shapes=[
            pltpu.SemaphoreType.DMA((2,)),
            pltpu.SemaphoreType.DMA((4, 2, n_z * n_y)),
            pltpu.SemaphoreType.DMA((2, n_z * n_y)),
        ],
        compiler_params=pltpu.CompilerParams(collective_id=0, has_side_effects=True),
    )(w_first, w_second)


def normalize(rows):
    wide = rows.astype(jnp.float32)
    scale = lax.rsqrt(jnp.mean(wide * wide, axis=-1, keepdims=True) + 1e-05)
    return wide * scale


def processor(stream, w_first, w_second):
    normed = normalize(stream).astype(jnp.bfloat16)
    hidden = jax.nn.silu(jnp.dot(normed, w_first, preferred_element_type=jnp.float32)).astype(
        jnp.bfloat16
    )
    branch = jnp.dot(hidden, w_second, preferred_element_type=jnp.float32)
    return (stream.astype(jnp.float32) + branch).astype(jnp.bfloat16)


def local(n_z, n_y, tokens, w_in, w_out, router, exp_in, exp_out, active_rows, active_expert):
    n_section = lax.axis_size("section")
    section = lax.axis_index("section")
    micro, tok_dev, width = tokens.shape
    rows_dev = micro * tok_dev
    part_width = width // n_section
    last = n_section - 1
    w_first, w_second = gather_weights(w_in[0], w_out[0], n_z, n_y)

    stream = tokens.reshape(rows_dev, width)
    for layer in range(n_section):
        stream = lax.cond(
            section == layer,
            lambda held: processor(held, w_first, w_second),
            lambda held: held,
            stream,
        )
        if layer < last:
            passed = lax.ppermute(stream, "section", [(layer, layer + 1)])
            stream = jnp.where(section == layer + 1, passed, stream)

    n_exp = router.shape[1]
    act_dev = active_rows.shape[0]
    capacity = -(-(3 * act_dev // n_exp) // 8) * 8
    chosen = active_expert[:, 0]
    same = chosen[:, None] == chosen[None, :]
    order = jnp.arange(act_dev, dtype=jnp.int32)
    rank = jnp.sum((same & (order[None, :] < order[:, None])).astype(jnp.int32), axis=1)
    position = chosen * capacity + rank
    places = n_exp * capacity
    onehot = chosen[:, None] == jnp.arange(n_exp, dtype=jnp.int32)[None, :]
    placing = jnp.arange(places, dtype=jnp.int32)[:, None] == position[None, :]
    picking = active_rows[:, None] == jnp.arange(rows_dev, dtype=jnp.int32)[None, :]
    placing = placing.astype(jnp.bfloat16)
    unplacing = jnp.dot(
        picking.T.astype(jnp.bfloat16), placing.T, preferred_element_type=jnp.float32
    ).astype(jnp.bfloat16)

    picked = jnp.dot(
        picking.astype(jnp.bfloat16), stream, preferred_element_type=jnp.float32
    ).astype(jnp.bfloat16)
    contact = normalize(picked).astype(jnp.bfloat16)
    both = jnp.concatenate([stream, contact], axis=0)
    mine = both[:, last * part_width :]
    for target in range(last):
        piece = both[:, target * part_width : (target + 1) * part_width]
        passed = lax.ppermute(piece, "section", [(last, target)])
        mine = jnp.where(section == target, passed, mine)
    base, contact = mine[:rows_dev], mine[rows_dev:]

    router_part = lax.dynamic_slice_in_dim(router, section * part_width, part_width, 0)
    logits = jnp.dot(contact, router_part, preferred_element_type=jnp.float32)
    logits = lax.psum(logits, "section")
    gate = jax.nn.sigmoid(jnp.sum(jnp.where(onehot, logits, 0.0), axis=1))
    gate_row = jnp.sum(jnp.where(picking, gate[:, None], 0.0), axis=0)

    outgoing = jnp.dot(placing, contact, preferred_element_type=jnp.float32).astype(jnp.bfloat16)
    outgoing = outgoing.reshape(n_exp, capacity, part_width)
    arrived = lax.all_to_all(outgoing, "expert", split_axis=0, concat_axis=0, tiled=True)
    rows = lax.all_gather(arrived.reshape(places, part_width), "section", axis=1, tiled=True)
    hidden = jax.nn.silu(jnp.dot(rows, exp_in[0], preferred_element_type=jnp.float32)).astype(
        jnp.bfloat16
    )
    partial_value = jnp.dot(hidden, exp_out[0], preferred_element_type=jnp.float32)
    summed = lax.psum_scatter(
        partial_value.astype(jnp.bfloat16), "section", scatter_dimension=1, tiled=True
    )
    returned = lax.all_to_all(
        summed.reshape(n_exp, capacity, part_width), "expert", split_axis=0, concat_axis=0, tiled=True
    ).reshape(places, part_width)
    value = jnp.dot(unplacing, returned, preferred_element_type=jnp.float32)
    mixed = base.astype(jnp.float32) + gate_row[:, None] * value
    return mixed.astype(jnp.bfloat16).reshape(micro, tok_dev, part_width)


def solution(mesh):
    n_y = mesh.shape["section"] // 2
    n_z = mesh.shape["expert"] // n_y
    return jax.shard_map(
        functools.partial(local, n_z, n_y),
        mesh=mesh,
        in_specs=(
            P(None, "expert", None),
            P("section", "expert", None),
            P("section", "expert", None),
            P(),
            P("expert", None, "section"),
            P("expert", "section", None),
            P("expert"),
            P("expert", None),
        ),
        out_specs=P(None, "expert", "section"),
        check_vma=False,
    )
```

time: 684 us -> 530 us (0.77)
  Pallas kernels: 0 us -> 250 us
  waiting for transfers between devices: 377 us -> 170 us
  starting transfers between devices: 85.8 us -> 15.2 us
  matrix products: 86.5 us -> 29.8 us
  other arithmetic: 42 us -> 11.7 us
  blocking collectives: 48.2 us -> 20.7 us
  local copies, waits for them, and re-layouts: 30 us -> 6.61 us
    pallas_call x0 -> x1, Pallas kernels: none -> 250 us  [gather_weights(): pl.pallas_call(functools.partial(gather_kernel, n_z, n_y), out_shape=(who...]
    all_gather x2 -> x1, waiting for transfers between devices: 254 us -> 19 us  [local(): lax.all_gather(arrived.reshape(places, part_width), 'section', axis=1, ti...]
    ppermute x11 -> x6, waiting for transfers between devices: 0.03 us -> 115 us  [the longest x3 112 us: local(): passed = lax.ppermute(piece, 'section', [(last, target)])]
    ppermute x11 -> x6, starting transfers between devices: 81.2 us -> 9.66 us  [the longest x3 6.96 us: local(): passed = lax.ppermute(stream, 'section', [(layer, layer + 1)])]
    psum x1 -> x0, waiting for transfers between devices: 61.8 us -> none  [spread(): return lax.psum(jnp.where(mine, shard, jnp.zeros_like(shard)), axis)]
    dot_general x8 -> x1, matrix products: 77.7 us -> 18.9 us  [processor(): branch = jnp.dot(hidden, w_second, preferred_element_type=jnp.float32)]
    all_to_all x1, waiting for transfers between devices: 41.3 us -> 5.97 us  [local(): lax.all_to_all(summed.reshape(n_exp, capacity, part_width), 'expert', spl...]
    all_to_all x1, blocking collectives: 48.2 us -> 14.6 us  [local(): lax.all_to_all(outgoing, 'expert', split_axis=0, concat_axis=0, tiled=True)]
  transfers between devices with their start and end apart: 16 -> 9, of which waited for: 5 -> 5; matrix products, arithmetic and copies ran while one was open for 3% -> 0% of each run, Pallas kernels for 0% -> 0%
where the time goes in v1:
time: 530 us; the launch traced here: 523 us
  Pallas kernels  250 us (47%)
  waiting for transfers between devices  170 us (32%)
  matrix products  29.8 us (6%)
  blocking collectives  20.7 us (4%)
  starting transfers between devices  15.2 us (3%)
  between operations  14 us (3%)
  other arithmetic  11.7 us (2%)
  local copies, waits for them, and re-layouts  6.61 us (1%)
    pallas_call x1, Pallas kernels, gather_weights(): pl.pallas_call(functools.partial(gather_kernel, n_z, n_y), out_shape=(who...  250 us
    ppermute x3, waiting for transfers between devices, local(): passed = lax.ppermute(piece, 'section', [(last, target)])  112 us
    reduce_scatter x1, waiting for transfers between devices, local(): lax.psum_scatter(partial_value.astype(jnp.bfloat16), 'section', scatter_d...  30 us
    all_gather x1, waiting for transfers between devices, local(): lax.all_gather(arrived.reshape(places, part_width), 'section', axis=1, ti...  19 us
    dot_general x1, matrix products, processor(): branch = jnp.dot(hidden, w_second, preferred_element_type=jnp.float32)  18.9 us
    all_to_all x1, blocking collectives, local(): lax.all_to_all(outgoing, 'expert', split_axis=0, concat_axis=0, tiled=True)  14.6 us
  transfers between devices with their start and end apart: 9, of which 5 were waited for; matrix products, arithmetic and copies ran while one was open for 0% of the time, Pallas kernels for 0%

profile of v1, /device:TPU:0, one launch (start us, length us, event | category | flops | bytes accessed | tf_op | source)
XLA Modules:
  0.0 523.1 jit_solution(2879546355007903931)
XLA Ops:
  6.5 3.5 copy.26
  10.1 250.4 %shard_map.82 = (bf16[2048,2048]{1,0:T(8,128)(2,1)}, bf16[2048,2048]{1,0:T(8,128)(2,1)}) custom-call(bf16[256,2048]{1,0:T(8,128)(2,1)} %bitcast.50, bf16[256,2048]{1,0:T(8,128)(2,1)} %bitcast.51), custom_call_target="tpu_custom_call" | custom-call | tf_op jit(solution)/shard_map/pallas_call | solution.py:98
  260.5 22.6 %conditional.4 = (bf16[576,2048]{1,0:T(8,128)(2,1)}) conditional(s32[]{:T(128)} %convert_element_type.100, bf16[576,2048]{1,0:T(8,128)(2,1)} %bitcast.46, (bf16[576,2048]{1,0:T(8,128)(2,1)}, bf16[2048,2048]{1,0:T(8,128)(2,1)}, bf16[2048,2048]{1,0:T(8,128)(2,1)}) %tuple.48), branch_computations={%region_0.0_spmd, %region_1.3_spmd} | conditional | flops 9680192512 | bytes 38020132 | solution.py:138
  260.5 1.7 copy.22
  262.2 1.4 copy-done.2
  263.6 0.5 fusion
  264.2 18.9 %fusion.2 = bf16[576,2048]{1,0:T(8,128)(2,1)} fusion(bf16[576,2048]{1,0:T(8,128)(2,1)} %copy-done.2, bf16[2048,2048]{1,0:T(8,128)(2,1)} %get-tuple-element.47, bf16[2048,2048]{1,0:T(8,128)(2,1)} %get-tuple-element.46, f32[576]{0:T(1024)S(1)} %add_rsqrt_fusion), kind=kOutput, calls=%fused_computation.5 | convolution fusion | flops 9676652544 | bytes 21498112 | tf_op jit(solution)/shard_map/cond/branch_1_fun/dot_general | solution.py:123
  283.1 2.7 collective-permute-start
  285.8 3.0 collective-permute-done
  288.9 3.3 broadcast_select_fusion
  292.3 2.1 collective-permute-start.1
  294.4 3.3 broadcast_select_fusion.1
  297.8 0.7 conditional.6
  298.4 2.1 collective-permute-start.2
  300.6 3.3 broadcast_select_fusion.2
  303.9 3.7 conditional.7
  307.6 2.6 multiply_reduce_fusion
  310.6 0.7 collective-permute-start.3
  311.3 0.7 collective-permute-start.4
  312.0 1.3 collective-permute-start.5
  313.6 112.0 %collective-permute-done.5 = bf16[720,512]{1,0:T(8,128)(2,1)S(1)} collective-permute-done((bf16[720,512]{1,0:T(8,128)(2,1)S(1)}, bf16[720,512]{1,0:T(8,128)(2,1)S(1)}, u32[]{:S(2)}, u32[]{:S(2)}) %collective-permute-start.5) | collective-permute-done | bytes 737312 | tf_op jit(solution)/shard_map/ppermute | solution.py:173
  425.6 0.5 fusion.45
  426.1 0.3 convolution_convert_fusion.3
  426.4 14.6 %all_to_all.10 = bf16[8,56,512]{2,1,0:T(8,128)(2,1)} all-to-all(bf16[8,56,512]{2,1,0:T(8,128)(2,1)S(1)} %bitcast.49), channel_id=1, replica_groups=mesh['section'=4,'expert'=8] {'expert'}, dimensions={0} | all-to-all | bytes 917504 | tf_op jit(solution)/shard_map/all_to_all | solution.py:185
  441.1 19.0 %all-gather.2.cloned.1.call-done = bf16[448,2048]{1,0:T(8,128)(2,1)} async-done(((bf16[448,512]{1,0:T(8,128)(2,1)}), bf16[448,2048]{1,0:T(8,128)(2,1)}) %all-gather.2.cloned.1.call-update) | async-done | bytes 1835024 | tf_op jit(solution)/shard_map/all_gather | solution.py:186
  460.1 5.6 %convolution_convert_fusion = bf16[448,2048]{1,0:T(8,128)(2,1)} fusion(bf16[1,512,2048]{2,1,0:T(8,128)(2,1)S(1)} %copy-done, bf16[448,2048]{1,0:T(8,128)(2,1)} %all-gather.2.cloned.1.call-done, bf16[1,2048,512]{2,1,0:T(8,128)(2,1)} %param.20), kind=kOutput, calls=%fused_computation.51 | convolution fusion | flops 1881112576 | bytes 7864320 | tf_op jit(solution)/shard_map/dot_general | solution.py:190
  465.7 30.0 %reduce-scatter.2.cloned.1.call-done = bf16[448,512]{1,0:T(8,128)(2,1)} async-done(((bf16[448,2048]{1,0:T(8,128)(2,1)}), bf16[448,512]{1,0:T(8,128)(2,1)}) %reduce-scatter.2.cloned.1.call-update) | async-done | bytes 458768 | tf_op jit(solution)/shard_map/reduce_scatter | solution.py:191
  495.7 5.5 %all-to-all-start.1 = ((bf16[8,56,512]{2,1,0:T(8,128)(2,1)}), bf16[8,56,512]{2,1,0:T(8,128)(2,1)S(1)}, u32[]{:S(2)}, u32[]{:S(2)}) async-start(bf16[8,56,512]{2,1,0:T(8,128)(2,1)} %bitcast.52), calls=%async_computation.2 | async-start | bytes 917504 | tf_op jit(solution)/shard_map/all_to_all | solution.py:194
  501.2 0.8 fusion.58
  502.0 6.1 %psum.7 = f32[144,8]{0,1:T(8,128)S(1)} all-reduce(f32[144,8]{0,1:T(8,128)S(1)} %fusion.58), channel_id=1, replica_groups=mesh['section'=4,'expert'=8] {'section'}, use_global_device_ids=true, to_apply=%region_13.14 | all-reduce | flops 1152 | bytes 9216 | tf_op jit(solution)/shard_map/psum | solution.py:179
  508.3 6.0 %all-to-all-done.1 = bf16[8,56,512]{2,1,0:T(8,128)(2,1)S(1)} async-done(((bf16[8,56,512]{2,1,0:T(8,128)(2,1)}), bf16[8,56,512]{2,1,0:T(8,128)(2,1)S(1)}, u32[]{:S(2)}, u32[]{:S(2)}) %all-to-all-start.1) | async-done | bytes 458784 | tf_op jit(solution)/shard_map/all_to_all | solution.py:194
  514.3 1.6 add_convert_fusion
  (27 shorter events, 1.0 us)
Async XLA Ops:
  6.5 453.6 %copy-start = (bf16[1,512,2048]{2,1,0:T(8,128)(2,1)S(1)}, bf16[1,512,2048]{2,1,0:T(8,128)(2,1)}, u32[]{:S(2)}) copy-start(bf16[1,512,2048]{2,1,0:T(8,128)(2,1)} %param.21) | copy-start | bytes 6291460
  6.5 453.6 %all-gather.2.cloned.1.call-start = ((), (), s32[]{:S(2)}) async-start(), calls=%async_computation.3 | async-start | bytes 2293760 | tf_op jit(solution)/shard_map/all_gather | solution.py:186
  262.2 1.4 copy-start.2
  283.1 5.8 %collective-permute-start = (bf16[576,2048]{1,0:T(8,128)(2,1)}, bf16[576,2048]{1,0:T(8,128)(2,1)}, u32[]{:S(2)}, u32[]{:S(2)}) collective-permute-start(bf16[576,2048]{1,0:T(8,128)(2,1)} %get-tuple-element.66), channel_id=1, source_target_pairs={{0,8},{1,9},{2,10},{3,11},{4,12},{5,13},{6,14},{7,15}} | collective-permute-start | bytes 7077896 | tf_op jit(solution)/shard_map/ppermute | solution.py:145
  292.3 2.1 collective-permute-start.1
  298.4 2.1 collective-permute-start.2
  303.9 3.7 copy-start.7
  307.6 2.8 copy-start.1
  310.4 2.9 copy-start.6
  310.6 2.9 collective-permute-start.3
  311.3 2.2 collective-permute-start.4
  312.0 113.6 %collective-permute-start.5 = (bf16[720,512]{1,0:T(8,128)(2,1)S(1)}, bf16[720,512]{1,0:T(8,128)(2,1)S(1)}, u32[]{:S(2)}, u32[]{:S(2)}) collective-permute-start(bf16[720,512]{1,0:T(8,128)(2,1)S(1)} %get-tuple-element.61), channel_id=1, source_target_pairs={{24,0},{25,1},{26,2},{27,3},{28,4},{29,5},{30,6},{31,7}} | collective-permute-start | bytes 2211848 | tf_op jit(solution)/shard_map/ppermute | solution.py:173
  441.0 54.7 %reduce-scatter.2.cloned.1.call-start = ((), (), s32[]{:S(2)}) async-start(), calls=%async_computation.4 | async-start | bytes 2293760 | tf_op jit(solution)/shard_map/reduce_scatter | solution.py:191
  495.7 18.6 %all-to-all-start.1 = ((bf16[8,56,512]{2,1,0:T(8,128)(2,1)}), bf16[8,56,512]{2,1,0:T(8,128)(2,1)S(1)}, u32[]{:S(2)}, u32[]{:S(2)}) async-start(bf16[8,56,512]{2,1,0:T(8,128)(2,1)} %bitcast.52), calls=%async_computation.2 | async-start | bytes 917504 | tf_op jit(solution)/shard_map/all_to_all | solution.py:194
Sparse Core Ops, SparseCore 0:
  441.1 18.9 all-gather.1
  465.8 29.7 reduce-scatter.1

commit v2 on v1

--- a/solution.py
+++ b/solution.py
@@ -133,17 +133,24 @@
     last = n_section - 1
     w_first, w_second = gather_weights(w_in[0], w_out[0], n_z, n_y)
 
-    stream = tokens.reshape(rows_dev, width)
-    for layer in range(n_section):
-        stream = lax.cond(
-            section == layer,
-            lambda held: processor(held, w_first, w_second),
-            lambda held: held,
-            stream,
-        )
-        if layer < last:
-            passed = lax.ppermute(stream, "section", [(layer, layer + 1)])
-            stream = jnp.where(section == layer + 1, passed, stream)
+    chunks = 2
+    streams = list(tokens.reshape(chunks, rows_dev // chunks, width))
+    for tick in range(chunks + last):
+        for index in range(chunks):
+            layer = tick - index
+            if not 0 <= layer <= last:
+                continue
+            stream = lax.cond(
+                section == layer,
+                lambda held: processor(held, w_first, w_second),
+                lambda held: held,
+                streams[index],
+            )
+            if layer < last:
+                passed = lax.ppermute(stream, "section", [(layer, layer + 1)])
+                stream = jnp.where(section == layer + 1, passed, stream)
+            streams[index] = stream
+    stream = jnp.concatenate(streams, axis=0)
 
     n_exp = router.shape[1]
     act_dev = active_rows.shape[0]

time: 530 us -> 514 us (0.970)
  waiting for transfers between devices: 170 us -> 147 us
    ppermute x3, waiting for transfers between devices: 112 us -> 92.7 us  [local(): passed = lax.ppermute(piece, 'section', [(last, target)])]
    dot_general x1 -> x2, matrix products: 18.9 us -> 24.2 us  [processor(): branch = jnp.dot(hidden, w_second, preferred_element_type=jnp.float32)]
    ppermute x3 -> x6, starting transfers between devices: 6.96 us -> 11.6 us  [local(): passed = lax.ppermute(stream, 'section', [(layer, layer + 1)])]
  transfers between devices with their start and end apart: 9 -> 12, of which waited for: 5 -> 4; matrix products, arithmetic and copies ran while one was open for 0% -> 4% of each run, Pallas kernels for 0% -> 0%
where the time goes in v2:
time: 514 us; the launch traced here: 506 us
  Pallas kernels  250 us (49%)
  waiting for transfers between devices  147 us (29%)
  matrix products  34.6 us (7%)
  blocking collectives  20.7 us (4%)
  starting transfers between devices  20.2 us (4%)
  between operations  14.1 us (3%)
  other arithmetic  8.91 us (2%)
  local copies, waits for them, and re-layouts  7.5 us (1%)
    pallas_call x1, Pallas kernels, gather_weights(): pl.pallas_call(functools.partial(gather_kernel, n_z, n_y), out_shape=(who...  250 us
    ppermute x3, waiting for transfers between devices, local(): passed = lax.ppermute(piece, 'section', [(last, target)])  92.7 us
    reduce_scatter x1, waiting for transfers between devices, local(): lax.psum_scatter(partial_value.astype(jnp.bfloat16), 'section', scatter_d...  30 us
    dot_general x2, matrix products, processor(): branch = jnp.dot(hidden, w_second, preferred_element_type=jnp.float32)  24.2 us
    all_gather x1, waiting for transfers between devices, local(): lax.all_gather(arrived.reshape(places, part_width), 'section', axis=1, ti...  18.7 us
    all_to_all x1, blocking collectives, local(): lax.all_to_all(outgoing, 'expert', split_axis=0, concat_axis=0, tiled=True)  14.6 us
    ppermute x6, starting transfers between devices, local(): passed = lax.ppermute(stream, 'section', [(layer, layer + 1)])  11.6 us
  transfers between devices with their start and end apart: 12, of which 4 were waited for; matrix products, arithmetic and copies ran while one was open for 4% of the time, Pallas kernels for 0%

profile of v2, /device:TPU:0, one launch (start us, length us, event | category | flops | bytes accessed | tf_op | source)
XLA Modules:
  0.0 506.3 jit_solution(3410461705147581441)
XLA Ops:
  6.5 3.0 fusion.128
  9.6 250.4 %shard_map.82 = (bf16[2048,2048]{1,0:T(8,128)(2,1)}, bf16[2048,2048]{1,0:T(8,128)(2,1)}) custom-call(bf16[256,2048]{1,0:T(8,128)(2,1)} %bitcast.44, bf16[256,2048]{1,0:T(8,128)(2,1)} %bitcast.45), custom_call_target="tpu_custom_call" | custom-call | tf_op jit(solution)/shard_map/pallas_call | solution.py:98
  260.0 15.3 %conditional.8 = (bf16[288,2048]{1,0:T(8,128)(2,1)}) conditional(s32[]{:T(128)} %convert_element_type.156, bf16[288,2048]{1,0:T(8,128)(2,1)} %bitcast.40, (bf16[288,2048]{1,0:T(8,128)(2,1)}, bf16[2048,2048]{1,0:T(8,128)(2,1)}, bf16[2048,2048]{1,0:T(8,128)(2,1)}) %tuple.86), branch_computations={%region_0.0_spmd, %region_1.3_spmd} | conditional | flops 4840096256 | bytes 27398692 | solution.py:143
  260.0 1.3 copy.33
  261.3 1.0 copy-done.6
  262.7 12.6 %fusion = bf16[288,2048]{1,0:T(8,128)(2,1)} fusion(bf16[2048,2048]{1,0:T(8,128)(2,1)} %get-tuple-element.87, bf16[288,2048]{1,0:T(8,128)(2,1)} %copy-done.6, bf16[2048,2048]{1,0:T(8,128)(2,1)} %get-tuple-element.86, f32[288]{0:T(512)S(1)} %add_rsqrt_fusion), kind=kOutput, calls=%fused_computation.3 | convolution fusion | flops 4838326272 | bytes 19137664 | tf_op jit(solution)/shard_map/cond/branch_1_fun/dot_general | solution.py:123
  275.3 2.3 collective-permute-start
  277.6 12.7 %conditional.12 = (bf16[288,2048]{1,0:T(8,128)(2,1)S(1)}) conditional(s32[]{:T(128)} %convert_element_type.156, bf16[288,2048]{1,0:T(8,128)(2,1)S(1)} %bitcast.38, (bf16[288,2048]{1,0:T(8,128)(2,1)S(1)}, bf16[2048,2048]{1,0:T(8,128)(2,1)}, bf16[2048,2048]{1,0:T(8,128)(2,1)}) %tuple.85), branch_computations={%region_12.13_spmd, %region_13.15_spmd} | conditional | flops 4840096256 | bytes 27398692 | solution.py:143
  278.7 11.6 %fusion.48 = bf16[288,2048]{1,0:T(8,128)(2,1)S(1)} fusion(bf16[2048,2048]{1,0:T(8,128)(2,1)} %get-tuple-element.99, bf16[288,2048]{1,0:T(8,128)(2,1)} %copy-done.7, bf16[2048,2048]{1,0:T(8,128)(2,1)} %get-tuple-element.98, f32[288]{0:T(512)S(1)} %add_rsqrt_fusion.4), kind=kOutput, calls=%fused_computation.51 | convolution fusion | flops 4838326272 | bytes 19137664 | tf_op jit(solution)/shard_map/cond/branch_1_fun/dot_general | solution.py:123
  290.3 2.3 collective-permute-start.3
  292.6 2.4 broadcast_select_fusion.1
  295.2 1.7 collective-permute-start.1
  296.9 1.2 broadcast_select_fusion
  298.0 1.8 collective-permute-start.4
  299.8 1.2 broadcast_select_fusion.3
  301.0 0.9 conditional.10
  301.9 1.7 collective-permute-start.2
  303.6 1.2 broadcast_select_fusion.2
  304.8 1.8 collective-permute-start.5
  306.6 1.1 broadcast_select_fusion.5
  308.4 1.3 conditional.11
  310.4 2.1 multiply_reduce_fusion
  314.7 1.3 collective-permute-start.8
  316.3 92.7 %collective-permute-done.8 = bf16[720,512]{1,0:T(8,128)(2,1)S(1)} collective-permute-done((bf16[720,512]{1,0:T(8,128)(2,1)S(1)}, bf16[720,512]{1,0:T(8,128)(2,1)S(1)}, u32[]{:S(2)}, u32[]{:S(2)}) %collective-permute-start.8) | collective-permute-done | bytes 737312 | tf_op jit(solution)/shard_map/ppermute | solution.py:180
  409.4 14.6 %all_to_all.10 = bf16[8,56,512]{2,1,0:T(8,128)(2,1)} all-to-all(bf16[8,56,512]{2,1,0:T(8,128)(2,1)S(1)} %bitcast.43), channel_id=1, replica_groups=mesh['section'=4,'expert'=8] {'expert'}, dimensions={0} | all-to-all | bytes 917504 | tf_op jit(solution)/shard_map/all_to_all | solution.py:192
  424.4 18.7 %all-gather.2.cloned.1.call-done = bf16[448,2048]{1,0:T(8,128)(2,1)} async-done(((bf16[448,512]{1,0:T(8,128)(2,1)}), bf16[448,2048]{1,0:T(8,128)(2,1)}) %all-gather.2.cloned.1.call-update) | async-done | bytes 1835024 | tf_op jit(solution)/shard_map/all_gather | solution.py:193
  443.2 5.6 %convolution_convert_fusion = bf16[448,2048]{1,0:T(8,128)(2,1)} fusion(bf16[1,512,2048]{2,1,0:T(8,128)(2,1)S(1)} %copy-done, bf16[448,2048]{1,0:T(8,128)(2,1)} %all-gather.2.cloned.1.call-done, bf16[1,2048,512]{2,1,0:T(8,128)(2,1)} %param.28), kind=kOutput, calls=%fused_computation.97 | convolution fusion | flops 1881112576 | bytes 7864320 | tf_op jit(solution)/shard_map/dot_general | solution.py:197
  448.8 30.0 %reduce-scatter.2.cloned.1.call-done = bf16[448,512]{1,0:T(8,128)(2,1)} async-done(((bf16[448,2048]{1,0:T(8,128)(2,1)}), bf16[448,512]{1,0:T(8,128)(2,1)}) %reduce-scatter.2.cloned.1.call-update) | async-done | bytes 458768 | tf_op jit(solution)/shard_map/reduce_scatter | solution.py:198
  478.8 5.5 %all-to-all-start.1 = ((bf16[8,56,512]{2,1,0:T(8,128)(2,1)}), bf16[8,56,512]{2,1,0:T(8,128)(2,1)S(1)}, u32[]{:S(2)}, u32[]{:S(2)}) async-start(bf16[8,56,512]{2,1,0:T(8,128)(2,1)} %bitcast.46), calls=%async_computation.2 | async-start | bytes 917504 | tf_op jit(solution)/shard_map/all_to_all | solution.py:201
  485.1 6.1 %psum.7 = f32[144,8]{0,1:T(8,128)S(1)} all-reduce(f32[144,8]{0,1:T(8,128)S(1)} %fusion.121), channel_id=1, replica_groups=mesh['section'=4,'expert'=8] {'section'}, use_global_device_ids=true, to_apply=%region_25.26 | all-reduce | flops 1152 | bytes 9216 | tf_op jit(solution)/shard_map/psum | solution.py:186
  491.4 6.0 %all-to-all-done.1 = bf16[8,56,512]{2,1,0:T(8,128)(2,1)S(1)} async-done(((bf16[8,56,512]{2,1,0:T(8,128)(2,1)}), bf16[8,56,512]{2,1,0:T(8,128)(2,1)S(1)}, u32[]{:S(2)}, u32[]{:S(2)}) %all-to-all-start.1) | async-done | bytes 458784 | tf_op jit(solution)/shard_map/all_to_all | solution.py:201
  497.4 1.6 add_convert_fusion
  (55 shorter events, 7.1 us)
Async XLA Ops:
  6.5 436.6 %copy-start = (bf16[1,512,2048]{2,1,0:T(8,128)(2,1)S(1)}, bf16[1,512,2048]{2,1,0:T(8,128)(2,1)}, u32[]{:S(2)}) copy-start(bf16[1,512,2048]{2,1,0:T(8,128)(2,1)} %param.29) | copy-start | bytes 6291460
  6.5 436.6 %all-gather.2.cloned.1.call-start = ((), (), s32[]{:S(2)}) async-start(), calls=%async_computation.3 | async-start | bytes 2293760 | tf_op jit(solution)/shard_map/all_gather | solution.py:193
  261.3 1.0 copy-start.6
  275.3 17.3 %collective-permute-start = (bf16[288,2048]{1,0:T(8,128)(2,1)}, bf16[288,2048]{1,0:T(8,128)(2,1)}, u32[]{:S(2)}, u32[]{:S(2)}) collective-permute-start(bf16[288,2048]{1,0:T(8,128)(2,1)} %get-tuple-element.120), channel_id=1, source_target_pairs={{0,8},{1,9},{2,10},{3,11},{4,12},{5,13},{6,14},{7,15}} | collective-permute-start | bytes 3538952 | tf_op jit(solution)/shard_map/ppermute | solution.py:150
  277.7 1.0 copy-start.7
  290.3 6.6 %collective-permute-start.3 = (bf16[288,2048]{1,0:T(8,128)(2,1)S(1)}, bf16[288,2048]{1,0:T(8,128)(2,1)}, u32[]{:S(2)}, u32[]{:S(2)}) collective-permute-start(bf16[288,2048]{1,0:T(8,128)(2,1)S(1)} %get-tuple-element.124), channel_id=1, source_target_pairs={{0,8},{1,9},{2,10},{3,11},{4,12},{5,13},{6,14},{7,15}} | collective-permute-start | bytes 3538952 | tf_op jit(solution)/shard_map/ppermute | solution.py:150
  295.2 4.7 collective-permute-start.1
  298.0 1.8 copy-start.2
  298.0 5.6 %collective-permute-start.4 = (bf16[288,2048]{1,0:T(8,128)(2,1)}, bf16[288,2048]{1,0:T(8,128)(2,1)}, u32[]{:S(2)}, u32[]{:S(2)}) collective-permute-start(bf16[288,2048]{1,0:T(8,128)(2,1)} %get-tuple-element.125), channel_id=1, source_target_pairs={{8,16},{9,17},{10,18},{11,19},{12,20},{13,21},{14,22},{15,23}} | collective-permute-start | bytes 3538952 | tf_op jit(solution)/shard_map/ppermute | solution.py:150
  301.0 2.6 copy-start.3
  301.9 4.7 collective-permute-start.2
  304.8 1.8 copy-start.4
  304.8 3.0 collective-permute-start.5
  306.6 1.7 copy-start.5
  309.8 0.7 copy-start.15
  310.4 2.3 copy-start.1
  313.1 2.9 copy-start.14
  313.3 2.9 collective-permute-start.6
  314.0 2.2 collective-permute-start.7
  314.7 94.2 %collective-permute-start.8 = (bf16[720,512]{1,0:T(8,128)(2,1)S(1)}, bf16[720,512]{1,0:T(8,128)(2,1)S(1)}, u32[]{:S(2)}, u32[]{:S(2)}) collective-permute-start(bf16[720,512]{1,0:T(8,128)(2,1)S(1)} %get-tuple-element.113), channel_id=1, source_target_pairs={{24,0},{25,1},{26,2},{27,3},{28,4},{29,5},{30,6},{31,7}} | collective-permute-start | bytes 2211848 | tf_op jit(solution)/shard_map/ppermute | solution.py:180
  424.1 54.7 %reduce-scatter.2.cloned.1.call-start = ((), (), s32[]{:S(2)}) async-start(), calls=%async_computation.4 | async-start | bytes 2293760 | tf_op jit(solution)/shard_map/reduce_scatter | solution.py:198
  478.8 18.6 %all-to-all-start.1 = ((bf16[8,56,512]{2,1,0:T(8,128)(2,1)}), bf16[8,56,512]{2,1,0:T(8,128)(2,1)S(1)}, u32[]{:S(2)}, u32[]{:S(2)}) async-start(bf16[8,56,512]{2,1,0:T(8,128)(2,1)} %bitcast.46), calls=%async_computation.2 | async-start | bytes 917504 | tf_op jit(solution)/shard_map/all_to_all | solution.py:201
Sparse Core Ops, SparseCore 0:
  424.2 18.9 all-gather.1
  448.9 29.7 reduce-scatter.1
